TPU v7x, 512 devices: a whole 4x4x16 slice. The times are simulated.
512 devices in a mesh: slab: 32 (over z, core), chan: 16 (over x, y).
Axes of the slice: x: 4, y: 4, z: 16, core: 2. Of those that a mesh axis runs over, the one named last changes fastest.
Arguments:
- image_center: bfloat16 [256, 256, 2048], P('slab', None, 'chan'), may hold values from -6 to 6
- image_radius: bfloat16 [256, 256, 2048], P('slab', None, 'chan'), may hold values from 4.976988e-06 to 4.9829483e-05
- first_kernel: bfloat16 [3, 3, 256, 256], replicated, may hold values from -0.125 to 0.125
- first_bias: float32 [256], replicated, may hold values from -3 to 3
- second_kernel: bfloat16 [3, 3, 256, 256], replicated, may hold values from -0.125 to 0.125
- second_bias: float32 [256], replicated, may hold values from -3 to 3
- third_weight: bfloat16 [256, 256], replicated, may hold values from -0.375 to 0.375
- third_bias: float32 [256], replicated, may hold values from -3 to 3
- fourth_weight: bfloat16 [256, 256], replicated, may hold values from -0.375 to 0.375
- fourth_bias: float32 [256], replicated, may hold values from -3 to 3
- score_weight: bfloat16 [256], replicated, may hold values from -0.375 to 0.375
- score_bias: float32 [1], replicated, may hold values from -3 to 3
- tile_count: int32 [32, 16], P('slab', 'chan'), may hold values from 0 to 2, as said below
- tile_row: int32 [32, 16, 2], P('slab', 'chan'), may hold values from 0 to 7, as said below
- owner_slot: int32 [32, 16, 2], P('slab', 'chan'), may hold values from -1 to 255, as said below
Outputs:
- ibp_bounds: float32 [2, 256, 2048], P(None, 'slab', 'chan')
- refined: float32 [256, 2, 128], P('slab')
Inputs may be any that keep to these rules, and one draw needn't show every extreme that they name: `tile_count`: each device holds 0 to 2 tiles in its first slots; in every draw some slab has 2 tiles on each of its devices, and the window holds exactly 256 tiles. `tile_row`: rows of the slots of one device are distinct; slots at or beyond the count are not used. `owner_slot`: slots below the count hold distinct global slots that cover all of 0 to 255; global slot g is kept by slab index g // 8; at most 1 tiles of one slab go to one slab index, and that many in every draw; slots at or beyond the count hold -1.
All inputs are finite; a program needn't handle non-finite values.
Results may differ from a plain program's by a relative error of at most 0.002.
The roundings to bfloat16 on the way count: a program that leaves them out, or rounds other values in their place, can miss the bound.
Values may be sent and summed in bfloat16 or wider, within the bound.
A program may use at most 64 MiB of HBM per device.

v0:
```python
import jax
import jax.numpy as jnp
from jax import lax
from jax.sharding import PartitionSpec as P

EPSILON = 1e-06


def extended(block, sides, width):
    for axis, dim in sides:
        count = lax.axis_size(axis)
        forward = [(i, i + 1) for i in range(count - 1)]
        backward = [(target, source) for source, target in forward]
        low = lax.ppermute(
            lax.slice_in_dim(block, block.shape[dim] - width, None, axis=dim), axis, forward
        )
        high = lax.ppermute(lax.slice_in_dim(block, 0, width, axis=dim), axis, backward)
        block = jnp.concatenate([low, block, high], axis=dim)
    return block


def interval_relu(center, radius):
    lower = jax.nn.relu(center - radius)
    upper = jax.nn.relu(center + radius)
    return (
        ((lower + upper) * 0.5).astype(jnp.bfloat16),
        ((upper - lower) * 0.5).astype(jnp.bfloat16),
    )


def relax_slopes(center, radius):
    upper = jax.nn.relu(center + radius)
    below = jax.nn.relu(radius - center)
    slope = upper / (upper + below + EPSILON)
    return (slope.astype(jnp.bfloat16), (slope * below).astype(jnp.bfloat16))


def conv_layer(middle, radius, kernel, layer_bias):
    row_count = middle.shape[0]
    col_count = middle.shape[2]
    padded = extended(jnp.stack([middle, radius]), (("slab", 1), ("chan", 3)), 1)
    magnitude = jnp.abs(kernel)
    center = jnp.zeros(middle.shape, jnp.float32)
    spread = jnp.zeros(middle.shape, jnp.float32)
    for row_shift in range(3):
        for col_shift in range(3):
            window_mid = padded[
                0, row_shift : row_shift + row_count, :, col_shift : col_shift + col_count
            ]
            window_rad = padded[
                1, row_shift : row_shift + row_count, :, col_shift : col_shift + col_count
            ]
            center = center + jnp.einsum(
                "oi,riw->row",
                kernel[row_shift, col_shift],
                window_mid,
                preferred_element_type=jnp.float32,
            )
            spread = spread + jnp.einsum(
                "oi,riw->row",
                magnitude[row_shift, col_shift],
                window_rad,
                preferred_element_type=jnp.float32,
            )
    return (center + layer_bias[None, :, None], spread)


def head_layer(middle, radius, weight, layer_bias):
    center = (
        jnp.einsum("oi,riw->row", weight, middle, preferred_element_type=jnp.float32)
        + layer_bias[None, :, None]
    )
    spread = jnp.einsum("oi,riw->row", jnp.abs(weight), radius, preferred_element_type=jnp.float32)
    return (center, spread)


def local_contract(coeffs, weight, first, width):
    return jnp.einsum("sjcp,cd->sjdp", coeffs, weight, preferred_element_type=jnp.float32)


def backward_bounds(
    tiles,
    first,
    width,
    contract,
    third_weight,
    third_bias,
    fourth_weight,
    fourth_bias,
    score_weight,
):
    signs = jnp.array([1.0, -1.0], jnp.float32)
    slope_three = tiles[:, 0].astype(jnp.float32)
    offset_three = tiles[:, 1].astype(jnp.float32)
    slope_four = tiles[:, 2].astype(jnp.float32)
    offset_four = tiles[:, 3].astype(jnp.float32)
    middle_two = tiles[:, 4].astype(jnp.float32)
    radius_two = tiles[:, 5].astype(jnp.float32)
    direction = signs[:, None] * score_weight.astype(jnp.float32)[None, :]
    coeff_four = (direction[:, None, :, None] * slope_four[None]).astype(jnp.bfloat16)
    constant = jnp.sum(
        jnp.minimum(direction, 0.0)[:, None, :, None] * offset_four[None]
        + coeff_four.astype(jnp.float32) * fourth_bias[None, None, :, None],
        axis=2,
    )
    carried = contract(coeff_four, fourth_weight, first, width)
    coeff_three = (carried * slope_three[None]).astype(jnp.bfloat16)
    constant = constant + jnp.sum(
        jnp.minimum(carried, 0.0) * offset_three[None]
        + coeff_three.astype(jnp.float32) * third_bias[None, None, :, None],
        axis=2,
    )
    reached = contract(coeff_three, third_weight, first, width)
    constant = constant + jnp.sum(
        reached * middle_two[None] - jnp.abs(reached) * radius_two[None], axis=2
    )
    return constant


def finish_bounds(total, score_bias):
    signs = jnp.array([1.0, -1.0], jnp.float32)
    lowest = total + signs[:, None, None] * score_bias[0]
    return jnp.stack([lowest[0], -lowest[1]], axis=1)


def owner_pack(values, owners, slab_count, pair_most, slot_cap):
    slot_total = owners.shape[0]
    present = owners >= 0
    target = jnp.where(present, owners // slot_cap, -1)
    place = jnp.where(present, owners % slot_cap, 0)
    ranks = jnp.arange(slot_total)
    earlier = (
        (target[:, None] == target[None, :]) & present[None, :] & (ranks[None, :] < ranks[:, None])
    )
    order = jnp.sum(earlier.astype(jnp.int32), axis=1)
    buffer_key = jnp.where(present, target * pair_most + order, -1)
    select = jnp.arange(slab_count * pair_most)[:, None] == buffer_key[None, :]
    packed = jnp.dot(
        select.astype(values.dtype),
        values.reshape(slot_total, -1),
        preferred_element_type=jnp.float32,
        precision=lax.Precision.HIGHEST,
    )
    packed = packed.reshape((slab_count, pair_most) + values.shape[1:])
    sent = jnp.sum(jnp.where(select, place[None, :] + 1, 0), axis=1) - 1
    return (packed, sent.reshape(slab_count, pair_most))


def owner_unpack(packed, sent, slot_cap):
    count = packed.shape[0] * packed.shape[1]
    flat = packed.reshape(count, -1)
    select = (jnp.arange(slot_cap)[:, None] == sent.reshape(-1)[None, :]).astype(packed.dtype)
    result = jnp.dot(
        select, flat, preferred_element_type=jnp.float32, precision=lax.Precision.HIGHEST
    )
    return result.reshape((slot_cap,) + packed.shape[2:])


def body(
    image_center,
    image_radius,
    first_kernel,
    first_bias,
    second_kernel,
    second_bias,
    third_weight,
    third_bias,
    fourth_weight,
    fourth_bias,
    score_weight,
    score_bias,
    tile_count,
    tile_row,
    owner_slot,
):
    tile_slots = tile_row.shape[-1]
    slab_count = lax.axis_size("slab")
    chan_count = lax.axis_size("chan")
    slot_cap = chan_count * tile_slots // 4
    pair_most = (chan_count * tile_slots + slab_count - 1) // slab_count
    middle_one, radius_one = interval_relu(
        *conv_layer(image_center, image_radius, first_kernel, first_bias)
    )
    middle_two, radius_two = interval_relu(
        *conv_layer(middle_one, radius_one, second_kernel, second_bias)
    )
    pre_three = head_layer(middle_two, radius_two, third_weight, third_bias)
    slope_three, offset_three = relax_slopes(*pre_three)
    middle_three, radius_three = interval_relu(*pre_three)
    pre_four = head_layer(middle_three, radius_three, fourth_weight, fourth_bias)
    slope_four, offset_four = relax_slopes(*pre_four)
    middle_four, radius_four = interval_relu(*pre_four)
    score_center = (
        jnp.einsum("c,rcw->rw", score_weight, middle_four, preferred_element_type=jnp.float32)
        + score_bias[0]
    )
    score_radius = jnp.einsum(
        "c,rcw->rw", jnp.abs(score_weight), radius_four, preferred_element_type=jnp.float32
    )
    ibp_bounds = jnp.stack([score_center - score_radius, score_center + score_radius])
    stacked = jnp.stack(
        [slope_three, offset_three, slope_four, offset_four, middle_two, radius_two], axis=1
    )
    tile_data = stacked[tile_row[0, 0]]
    owners_here = jnp.where(jnp.arange(tile_slots) < tile_count[0, 0], owner_slot[0, 0], -1)
    layer_args = (third_weight, third_bias, fourth_weight, fourth_bias, score_weight)
    total = backward_bounds(tile_data, 0, tile_data.shape[2], local_contract, *layer_args)
    bounds = finish_bounds(total, score_bias)
    packed, sent = owner_pack(bounds, owners_here, slab_count, pair_most, slot_cap)
    arrived, arrived_slots = (
        lax.all_to_all(packed, "slab", split_axis=0, concat_axis=0, tiled=True),
        lax.all_to_all(sent, "slab", split_axis=0, concat_axis=0, tiled=True),
    )
    refined = lax.psum(owner_unpack(arrived, arrived_slots, slot_cap), "chan")
    return (ibp_bounds, refined)


def solution(mesh):
    placed = (
        P("slab", None, "chan"),
        P("slab", None, "chan"),
        P(),
        P(),
        P(),
        P(),
        P(),
        P(),
        P(),
        P(),
        P(),
        P(),
        P("slab", "chan"),
        P("slab", "chan", None),
        P("slab", "chan", None),
    )
    return jax.shard_map(
        body,
        mesh=mesh,
        in_specs=placed,
        out_specs=(P(None, "slab", "chan"), P("slab", None, None)),
        check_vma=False,
    )
```

profile of v0, /device:TPU:32, one launch (start us, length us, event | category | flops | bytes accessed | tf_op | source)
XLA Modules:
  0.0 155.9 jit_solution(16238189483117431858)
XLA Ops:
  0.6 1.3 copy.47
  2.9 1.9 %collective-permute-start = (bf16[2,1,256,128]{2,3,1,0:T(8,128)(2,1)}, bf16[2,1,256,128]{2,3,1,0:T(8,128)(2,1)S(1)}, u32[]{:S(2)}, u32[]{:S(2)}) collective-permute-start(bf16[2,1,256,128]{2,3,1,0:T(8,128)(2,1)} %get-tuple-element.26), channel_id=1, source_target_pairs={{0,16},{16,32},{32,48},{48,64},{64,80},{80,96},{96,112},{112,128},... | collective-permute-start | bytes 393224 | tf_op jit(solution)/shard_map/ppermute | solution.py:14
  4.9 3.6 %collective-permute-start.1 = (bf16[2,1,256,128]{2,3,1,0:T(8,128)(2,1)}, bf16[2,1,256,128]{2,3,1,0:T(8,128)(2,1)}, u32[]{:S(2)}, u32[]{:S(2)}) collective-permute-start(bf16[2,1,256,128]{2,3,1,0:T(8,128)(2,1)} %get-tuple-element.27), channel_id=1, source_target_pairs={{16,0},{32,16},{48,32},{64,48},{80,64},{96,80},{112,96},{128,112},... | collective-permute-start | bytes 393224 | tf_op jit(solution)/shard_map/ppermute | solution.py:17
  10.2 16.6 %all-to-all-start = ((s32[32,1,1]{2,1,0:T(1,128)}), s32[32,1,1]{2,1,0:T(1,128)S(1)}, u32[]{:S(2)}, u32[]{:S(2)}) async-start(s32[32,1,1]{2,1,0:T(1,128)} %copy.51), calls=%async_computation | async-start | bytes 32768 | tf_op jit(solution)/shard_map/all_to_all | solution.py:212
  26.8 1.3 fusion.138
  29.2 1.3 fusion.122
  33.6 1.3 abs.19
  35.4 2.6 %all-to-all-done = s32[32,1,1]{2,1,0:T(1,128)S(1)} async-done(((s32[32,1,1]{2,1,0:T(1,128)}), s32[32,1,1]{2,1,0:T(1,128)S(1)}, u32[]{:S(2)}, u32[]{:S(2)}) %all-to-all-start) | async-done | bytes 160 | tf_op jit(solution)/shard_map/all_to_all | solution.py:212
  38.0 1.2 reduce
  40.0 3.6 %collective-permute-start.2 = (bf16[2,10,256,1]{2,3,1,0:T(2,128)(2,1)S(1)}, bf16[2,10,256,1]{2,3,1,0:T(2,128)(2,1)S(1)}, u32[]{:S(2)}, u32[]{:S(2)}) collective-permute-start(bf16[2,10,256,1]{2,3,1,0:T(2,128)(2,1)S(1)} %get-tuple-element.22), channel_id=1, source_target_pairs={{0,1},{1,2},{2,3},{3,4},{4,5},{5,6},{6,7},{7,8},{8,9},{9,10},{10,1... | collective-permute-start | bytes 30728 | tf_op jit(solution)/shard_map/ppermute | solution.py:14
  43.6 1.3 collective-permute-start.3
  45.6 1.2 fusion.79
  46.7 1.2 fusion.90
  47.9 1.3 collective-permute-done.3
  49.3 1.7 %maximum_maximum_fusion = (bf16[2,10,256,129]{2,3,1,0:T(8,128)(2,1)S(1)}, bf16[2,10,256,129]{2,3,1,0:T(8,128)(2,1)S(1)}) fusion(bf16[2,1,256,128]{2,3,1,0:T(8,128)(2,1)} %collective-permute-done.1, bf16[1,8,256,128]{2,3,1,0:T(8,128)(2,1)S(1)} %bitcast.571, bf16[1,8,256,128]{2,3,1,0:T(8,128)(2,1)S(1)} %bitcast.564, ...), kind=kLoop, calls=%fused_computation.1 | loop fusion | flops 13209600 | bytes 3973120 | tf_op jit(solution)/shard_map/concatenate | solution.py:18
  54.6 0.8 copy-done.5
  57.6 1.9 %collective-permute-start.4 = (bf16[2,1,256,128]{2,3,1,0:T(8,128)(2,1)S(1)}, bf16[2,1,256,128]{2,3,1,0:T(8,128)(2,1)S(1)}, u32[]{:S(2)}, u32[]{:S(2)}) collective-permute-start(bf16[2,1,256,128]{2,3,1,0:T(8,128)(2,1)S(1)} %get-tuple-element.24), channel_id=1, source_target_pairs={{0,16},{16,32},{32,48},{48,64},{64,80},{80,96},{96,112},{112,128},... | collective-permute-start | bytes 393224 | tf_op jit(solution)/shard_map/ppermute | solution.py:14
  59.5 3.6 %collective-permute-start.5 = (bf16[2,1,256,128]{2,3,1,0:T(8,128)(2,1)S(1)}, bf16[2,1,256,128]{2,3,1,0:T(8,128)(2,1)S(1)}, u32[]{:S(2)}, u32[]{:S(2)}) collective-permute-start(bf16[2,1,256,128]{2,3,1,0:T(8,128)(2,1)S(1)} %get-tuple-element.25), channel_id=1, source_target_pairs={{16,0},{32,16},{48,32},{64,48},{80,64},{96,80},{112,96},{128,112},... | collective-permute-start | bytes 393224 | tf_op jit(solution)/shard_map/ppermute | solution.py:17
  63.9 1.8 %collective-permute-done.5 = bf16[2,1,256,128]{2,3,1,0:T(8,128)(2,1)S(1)} collective-permute-done((bf16[2,1,256,128]{2,3,1,0:T(8,128)(2,1)S(1)}, bf16[2,1,256,128]{2,3,1,0:T(8,128)(2,1)S(1)}, u32[]{:S(2)}, u32[]{:S(2)}) %collective-permute-start.5) | collective-permute-done | bytes 131104 | tf_op jit(solution)/shard_map/ppermute | solution.py:17
  65.7 3.5 %collective-permute-start.6 = (bf16[2,10,256,1]{2,3,1,0:T(2,128)(2,1)S(1)}, bf16[2,10,256,1]{2,3,1,0:T(2,128)(2,1)S(1)}, u32[]{:S(2)}, u32[]{:S(2)}) collective-permute-start(bf16[2,10,256,1]{2,3,1,0:T(2,128)(2,1)S(1)} %get-tuple-element.18), channel_id=1, source_target_pairs={{0,1},{1,2},{2,3},{3,4},{4,5},{5,6},{6,7},{7,8},{8,9},{9,10},{10,1... | collective-permute-start | bytes 30728 | tf_op jit(solution)/shard_map/ppermute | solution.py:14
  69.2 1.5 collective-permute-start.7
  72.1 2.8 %collective-permute-done.7 = bf16[2,10,256,1]{2,3,1,0:T(2,128)(2,1)S(1)} collective-permute-done((bf16[2,10,256,1]{2,3,1,0:T(2,128)(2,1)S(1)}, bf16[2,10,256,1]{2,3,1,0:T(2,128)(2,1)S(1)}, u32[]{:S(2)}, u32[]{:S(2)}) %collective-permute-start.7) | collective-permute-done | bytes 10272 | tf_op jit(solution)/shard_map/ppermute | solution.py:17
  81.0 1.3 bitcast_dynamic-update-slice_fusion.3
  82.3 1.2 fusion.48
  83.9 1.3 bitcast_dynamic-update-slice_fusion.2
  85.3 1.1 fusion.50
  86.4 0.8 bitcast_dynamic-update-slice_fusion.1
  87.2 0.8 bitcast_dynamic-update-slice_fusion
  88.0 2.6 %gather_fusion = bf16[2,6,256,128]{2,3,1,0:T(8,128)(2,1)S(1)} fusion(bf16[8,6,256,128]{2,3,0,1:T(8,128)(2,1)} %bitcast_dynamic-update-slice_fusion, s32[1024]{0:T(1024)} %pad_clamp_fusion), kind=kCustom, calls=%fused_computation | custom fusion | bytes 1572872 | tf_op jit(solution)/shard_map/gather | solution.py:204
  93.3 10.8 %all-to-all-start.1 = ((f32[32,1,2,128]{3,2,1,0:T(2,128)}), f32[32,1,2,128]{3,2,1,0:T(2,128)S(1)}, u32[]{:S(2)}, u32[]{:S(2)}) async-start(f32[32,1,2,128]{3,2,1,0:T(2,128)} %copy.52), calls=%async_computation.1 | async-start | bytes 65536 | tf_op jit(solution)/shard_map/all_to_all | solution.py:211
  105.5 10.5 %all-to-all-done.1 = f32[32,1,2,128]{3,2,1,0:T(2,128)S(1)} async-done(((f32[32,1,2,128]{3,2,1,0:T(2,128)}), f32[32,1,2,128]{3,2,1,0:T(2,128)S(1)}, u32[]{:S(2)}, u32[]{:S(2)}) %all-to-all-start.1) | async-done | bytes 32800 | tf_op jit(solution)/shard_map/all_to_all | solution.py:211
  116.1 39.2 %psum.7 = f32[8,2,128]{2,0,1:T(8,128)S(1)} all-reduce(f32[8,2,128]{2,0,1:T(8,128)S(1)} %fusion.168), channel_id=1, replica_groups=mesh['slab'=32,'chan'=16] {'chan'}, use_global_device_ids=true, to_apply=%region_5.6 | all-reduce | flops 2048 | bytes 16384 | tf_op jit(solution)/shard_map/psum | solution.py:214
  (129 shorter events, 26.4 us)
Async XLA Ops:
  0.6 1.3 copy-start.8
  2.0 7.2 %copy-start.21 = (s32[1,1,2]{2,1,0:T(1,128)S(1)}, s32[1,1,2]{2,1,0:T(1,128)}, u32[]{:S(2)}) copy-start(s32[1,1,2]{2,1,0:T(1,128)} %param.31) | copy-start | bytes 28
  2.0 24.8 %copy-start = (bf16[3,3,256,256]{3,2,1,0:T(8,128)(2,1)S(1)}, bf16[3,3,256,256]{3,2,1,0:T(8,128)(2,1)}, u32[]{:S(2)}) copy-start(bf16[3,3,256,256]{3,2,1,0:T(8,128)(2,1)} %param.19) | copy-start | bytes 3538948
  2.0 24.8 %copy-start.7 = (bf16[8,256,128]{2,1,0:T(8,128)(2,1)S(1)}, bf16[8,256,128]{2,1,0:T(8,128)(2,1)}, u32[]{:S(2)}) copy-start(bf16[8,256,128]{2,1,0:T(8,128)(2,1)} %param.17) | copy-start | bytes 1572868
  2.9 36.2 %collective-permute-start = (bf16[2,1,256,128]{2,3,1,0:T(8,128)(2,1)}, bf16[2,1,256,128]{2,3,1,0:T(8,128)(2,1)S(1)}, u32[]{:S(2)}, u32[]{:S(2)}) collective-permute-start(bf16[2,1,256,128]{2,3,1,0:T(8,128)(2,1)} %get-tuple-element.26), channel_id=1, source_target_pairs={{0,16},{16,32},{32,48},{48,64},{64,80},{80,96},{96,112},{112,128},... | collective-permute-start | bytes 393224 | tf_op jit(solution)/shard_map/ppermute | solution.py:14
  4.9 34.3 %collective-permute-start.1 = (bf16[2,1,256,128]{2,3,1,0:T(8,128)(2,1)}, bf16[2,1,256,128]{2,3,1,0:T(8,128)(2,1)}, u32[]{:S(2)}, u32[]{:S(2)}) collective-permute-start(bf16[2,1,256,128]{2,3,1,0:T(8,128)(2,1)} %get-tuple-element.27), channel_id=1, source_target_pairs={{16,0},{32,16},{48,32},{64,48},{80,64},{96,80},{112,96},{128,112},... | collective-permute-start | bytes 393224 | tf_op jit(solution)/shard_map/ppermute | solution.py:17
  9.4 18.7 %copy-start.22 = (s32[2]{0:T(128)}, s32[2]{0:T(128)S(1)}, u32[]{:S(2)}) copy-start(s32[2]{0:T(128)S(1)} %get-tuple-element.41) | copy-start | bytes 28
  10.2 27.8 %all-to-all-start = ((s32[32,1,1]{2,1,0:T(1,128)}), s32[32,1,1]{2,1,0:T(1,128)S(1)}, u32[]{:S(2)}, u32[]{:S(2)}) async-start(s32[32,1,1]{2,1,0:T(1,128)} %copy.51), calls=%async_computation | async-start | bytes 32768 | tf_op jit(solution)/shard_map/all_to_all | solution.py:212
  28.1 1.0 copy-start.9
  29.2 5.7 %copy-start.3 = (bf16[3,3,256,256]{3,2,1,0:T(8,128)(2,1)}, bf16[3,3,256,256]{3,2,1,0:T(8,128)(2,1)S(1)}, u32[]{:S(2)}) copy-start(bf16[3,3,256,256]{3,2,1,0:T(8,128)(2,1)S(1)} %abs.18) | copy-start | bytes 3538948
  29.2 1.3 copy-start.27
  29.2 1.3 copy-start.25
  29.2 2.0 %copy-start.26 = (f32[2]{0:T(128)S(1)}, f32[2]{0:T(128)}, u32[]{:S(2)}) copy-start(f32[2]{0:T(128)} %constant.58.clone) | copy-start | bytes 28
  29.2 4.4 %copy-start.1 = (bf16[3,3,256,256]{3,2,1,0:T(8,128)(2,1)S(1)}, bf16[3,3,256,256]{3,2,1,0:T(8,128)(2,1)}, u32[]{:S(2)}) copy-start(bf16[3,3,256,256]{3,2,1,0:T(8,128)(2,1)} %param.21) | copy-start | bytes 3538948
  39.9 5.3 %copy-start.4 = (bf16[3,3,256,256]{3,2,1,0:T(8,128)(2,1)S(1)}, bf16[3,3,256,256]{3,2,1,0:T(8,128)(2,1)}, u32[]{:S(2)}) copy-start(bf16[3,3,256,256]{3,2,1,0:T(8,128)(2,1)} %copy-done.3) | copy-start | bytes 3538948
  40.0 8.0 %collective-permute-start.2 = (bf16[2,10,256,1]{2,3,1,0:T(2,128)(2,1)S(1)}, bf16[2,10,256,1]{2,3,1,0:T(2,128)(2,1)S(1)}, u32[]{:S(2)}, u32[]{:S(2)}) collective-permute-start(bf16[2,10,256,1]{2,3,1,0:T(2,128)(2,1)S(1)} %get-tuple-element.22), channel_id=1, source_target_pairs={{0,1},{1,2},{2,3},{3,4},{4,5},{5,6},{6,7},{7,8},{8,9},{9,10},{10,1... | collective-permute-start | bytes 30728 | tf_op jit(solution)/shard_map/ppermute | solution.py:14
  43.6 5.7 %collective-permute-start.3 = (bf16[2,10,256,1]{2,3,1,0:T(2,128)(2,1)S(1)}, bf16[2,10,256,1]{2,3,1,0:T(2,128)(2,1)S(1)}, u32[]{:S(2)}, u32[]{:S(2)}) collective-permute-start(bf16[2,10,256,1]{2,3,1,0:T(2,128)(2,1)S(1)} %get-tuple-element.23), channel_id=1, source_target_pairs={{1,0},{2,1},{3,2},{4,3},{5,4},{6,5},{7,6},{8,7},{9,8},{10,9},{11,1... | collective-permute-start | bytes 30728 | tf_op jit(solution)/shard_map/ppermute | solution.py:17
  53.0 1.2 copy-start.6
  54.2 1.2 copy-start.5
  57.2 6.0 %copy-start.2 = (bf16[3,3,256,256]{3,2,1,0:T(8,128)(2,1)S(1)}, bf16[3,3,256,256]{3,2,1,0:T(8,128)(2,1)}, u32[]{:S(2)}) copy-start(bf16[3,3,256,256]{3,2,1,0:T(8,128)(2,1)} %abs.19) | copy-start | bytes 3538948
  57.6 6.3 %collective-permute-start.4 = (bf16[2,1,256,128]{2,3,1,0:T(8,128)(2,1)S(1)}, bf16[2,1,256,128]{2,3,1,0:T(8,128)(2,1)S(1)}, u32[]{:S(2)}, u32[]{:S(2)}) collective-permute-start(bf16[2,1,256,128]{2,3,1,0:T(8,128)(2,1)S(1)} %get-tuple-element.24), channel_id=1, source_target_pairs={{0,16},{16,32},{32,48},{48,64},{64,80},{80,96},{96,112},{112,128},... | collective-permute-start | bytes 393224 | tf_op jit(solution)/shard_map/ppermute | solution.py:14
  59.5 6.1 %collective-permute-start.5 = (bf16[2,1,256,128]{2,3,1,0:T(8,128)(2,1)S(1)}, bf16[2,1,256,128]{2,3,1,0:T(8,128)(2,1)S(1)}, u32[]{:S(2)}, u32[]{:S(2)}) collective-permute-start(bf16[2,1,256,128]{2,3,1,0:T(8,128)(2,1)S(1)} %get-tuple-element.25), channel_id=1, source_target_pairs={{16,0},{32,16},{48,32},{64,48},{80,64},{96,80},{112,96},{128,112},... | collective-permute-start | bytes 393224 | tf_op jit(solution)/shard_map/ppermute | solution.py:17
  65.7 6.4 %collective-permute-start.6 = (bf16[2,10,256,1]{2,3,1,0:T(2,128)(2,1)S(1)}, bf16[2,10,256,1]{2,3,1,0:T(2,128)(2,1)S(1)}, u32[]{:S(2)}, u32[]{:S(2)}) collective-permute-start(bf16[2,10,256,1]{2,3,1,0:T(2,128)(2,1)S(1)} %get-tuple-element.18), channel_id=1, source_target_pairs={{0,1},{1,2},{2,3},{3,4},{4,5},{5,6},{6,7},{7,8},{8,9},{9,10},{10,1... | collective-permute-start | bytes 30728 | tf_op jit(solution)/shard_map/ppermute | solution.py:14
  69.2 5.7 %collective-permute-start.7 = (bf16[2,10,256,1]{2,3,1,0:T(2,128)(2,1)S(1)}, bf16[2,10,256,1]{2,3,1,0:T(2,128)(2,1)S(1)}, u32[]{:S(2)}, u32[]{:S(2)}) collective-permute-start(bf16[2,10,256,1]{2,3,1,0:T(2,128)(2,1)S(1)} %get-tuple-element.19), channel_id=1, source_target_pairs={{1,0},{2,1},{3,2},{4,3},{5,4},{6,5},{7,6},{8,7},{9,8},{10,9},{11,1... | collective-permute-start | bytes 30728 | tf_op jit(solution)/shard_map/ppermute | solution.py:17
  79.8 0.9 copy-start.11
  79.8 0.9 copy-start.15
  82.3 1.2 copy-start.10
  82.3 1.2 copy-start.14
  91.5 12.6 %copy-start.19 = (bf16[256,1,1]{0,1,2:T(2,128)(2,1)S(1)}, bf16[256,1,1]{0,1,2:T(2,128)(2,1)}, u32[]{:S(2)}) copy-start(bf16[256,1,1]{0,1,2:T(2,128)(2,1)} %reshape.313) | copy-start | bytes 1540
  92.3 12.2 %copy-start.20 = (bf16[256,1,1]{0,1,2:T(2,128)(2,1)S(1)}, bf16[256,1,1]{0,1,2:T(2,128)(2,1)}, u32[]{:S(2)}) copy-start(bf16[256,1,1]{0,1,2:T(2,128)(2,1)} %reshape.315) | copy-start | bytes 1540
  93.3 22.6 %all-to-all-start.1 = ((f32[32,1,2,128]{3,2,1,0:T(2,128)}), f32[32,1,2,128]{3,2,1,0:T(2,128)S(1)}, u32[]{:S(2)}, u32[]{:S(2)}) async-start(f32[32,1,2,128]{3,2,1,0:T(2,128)} %copy.52), calls=%async_computation.1 | async-start | bytes 65536 | tf_op jit(solution)/shard_map/all_to_all | solution.py:211
  104.5 11.4 %copy-start.16 = (s32[32]{0:T(128)S(1)}, s32[32]{0:T(128)}, u32[]{:S(2)}) copy-start(s32[32]{0:T(128)} %reduce) | copy-start | bytes 388
  (6 other events, 4.3 us)
where the time goes:
time: 157 us; the launch traced here: 156 us
  starting transfers between devices  48.4 us (31%)
  blocking collectives  39.2 us (25%)
  matrix products  22 us (14%)
  waiting for transfers between devices  19.3 us (12%)
  local copies, waits for them, and re-layouts  12.4 us (8%)
  other arithmetic  12.1 us (8%)
  between operations  2.5 us (2%)
    psum x1, blocking collectives, body(): refined = lax.psum(owner_unpack(arrived, arrived_slots, slot_cap), 'chan')  39.2 us
    all_to_all x1, starting transfers between devices, body(): lax.all_to_all(sent, 'slab', split_axis=0, concat_axis=0, tiled=True)  16.6 us
    ppermute x4, starting transfers between devices, extended(): lax.ppermute(lax.slice_in_dim(block, block.shape[dim] - width, None, axis...  10.9 us
    all_to_all x1, starting transfers between devices, body(): lax.all_to_all(packed, 'slab', split_axis=0, concat_axis=0, tiled=True)  10.8 us
    all_to_all x1, waiting for transfers between devices, body(): lax.all_to_all(packed, 'slab', split_axis=0, concat_axis=0, tiled=True)  10.5 us
    ppermute x4, starting transfers between devices, extended(): lax.ppermute(lax.slice_in_dim(block, 0, width, axis=dim), axis, backward)  10 us
    dot_general x18, matrix products, conv_layer(): jnp.einsum('oi,riw->row', kernel[row_shift, col_shift], window_mid, prefe...  8.74 us
    dot_general x18, matrix products, conv_layer(): jnp.einsum('oi,riw->row', magnitude[row_shift, col_shift], window_rad, pr...  8.11 us
  transfers between devices with their start and end apart: 10, of which 6 were waited for; matrix products, arithmetic and copies ran while one was open for 10% of the time, Pallas kernels for 0%

commit v1 on v0

v1 whole, which is shorter than its diff:
```python
import functools

import jax
import jax.numpy as jnp
from jax import lax
from jax.experimental import pallas as pl
from jax.experimental.pallas import tpu as pltpu
from jax.sharding import PartitionSpec as P

EPSILON = 1e-06
MESH = pl.DeviceIdType.MESH
BF = jnp.bfloat16
F32 = jnp.float32
C = 256
PIX = 128
ROWS = 8
PAD = 144


def dot_nt(lhs, rhs):
    return lax.dot_general(lhs, rhs, (((1,), (1,)), ((), ())), preferred_element_type=F32)


def dot_nn(lhs, rhs):
    return lax.dot_general(lhs, rhs, (((1,), (0,)), ((), ())), preferred_element_type=F32)


def interval_relu(center, radius):
    lower = jnp.maximum(center - radius, 0.0)
    upper = jnp.maximum(center + radius, 0.0)
    return (lower + upper) * 0.5, (upper - lower) * 0.5


def relax_slopes(center, radius):
    upper = jnp.maximum(center + radius, 0.0)
    below = jnp.maximum(radius - center, 0.0)
    slope = upper / (upper + below + EPSILON)
    return slope.astype(BF).astype(F32), (slope * below).astype(BF).astype(F32)


def kernel(
    n_slab,
    n_chan,
    center_in,
    radius_in,
    first_in,
    second_in,
    third_in,
    fourth_in,
    first_bias,
    second_bias,
    third_bias,
    fourth_bias,
    score_weight,
    score_bias,
    tile_count,
    tile_row,
    owner_slot,
    ibp_out,
    refined_out,
    raw,
    wide,
    side,
    layer,
    first,
    second,
    third,
    fourth,
    gathered,
    message,
    arrived,
    local_sem,
    halo_send,
    halo_recv,
    chan_send,
    chan_recv,
    slab_send,
    slab_recv,
):
    s = lax.axis_index("slab")
    c = lax.axis_index("chan")

    def slab_at(step):
        return lax.rem(s + step + n_slab, n_slab)

    def chan_at(step):
        return lax.rem(c + step + n_chan, n_chan)

    loads = [
        pltpu.make_async_copy(center_in, raw.at[0, pl.ds(2, ROWS)], local_sem.at[0]),
        pltpu.make_async_copy(radius_in, raw.at[1, pl.ds(2, ROWS)], local_sem.at[1]),
        pltpu.make_async_copy(first_in, first, local_sem.at[2]),
        pltpu.make_async_copy(second_in, second, local_sem.at[3]),
        pltpu.make_async_copy(third_in, third, local_sem.at[4]),
        pltpu.make_async_copy(fourth_in, fourth, local_sem.at[5]),
    ]
    for load in loads:
        load.start()

    barrier = pltpu.get_barrier_semaphore()

    def greet_chan(step, carry):
        pl.semaphore_signal(
            barrier, inc=1, device_id=(s, chan_at(step)), device_id_type=MESH
        )
        return carry

    def greet_slab(step, carry):
        pl.semaphore_signal(
            barrier, inc=1, device_id=(slab_at(step), c), device_id_type=MESH
        )
        return carry

    for row_step in (-1, 1):
        for col_step in (-1, 1):
            pl.semaphore_signal(
                barrier,
                inc=1,
                device_id=(slab_at(row_step), chan_at(col_step)),
                device_id_type=MESH,
            )
    lax.fori_loop(1, n_chan, greet_chan, 0)
    lax.fori_loop(1, n_slab, greet_slab, 0)
    pl.semaphore_wait(barrier, n_chan + n_slab + 2)

    def send(index, source, target, row_step, col_step):
        copy = pltpu.make_async_remote_copy(
            src_ref=source,
            dst_ref=target,
            send_sem=halo_send.at[index],
            recv_sem=halo_recv.at[index],
            device_id=(slab_at(row_step), chan_at(col_step)),
            device_id_type=MESH,
        )
        copy.start()
        return copy

    row_copies = [
        send(0, center_in.at[pl.ds(6, 2)], raw.at[0, pl.ds(0, 2)], 1, 0),
        send(1, center_in.at[pl.ds(0, 2)], raw.at[0, pl.ds(10, 2)], -1, 0),
        send(2, radius_in.at[pl.ds(6, 2)], raw.at[1, pl.ds(0, 2)], 1, 0),
        send(3, radius_in.at[pl.ds(0, 2)], raw.at[1, pl.ds(10, 2)], -1, 0),
    ]

    place = lax.broadcasted_iota(jnp.int32, (3, PAD, PIX), 1)
    shift = lax.broadcasted_iota(jnp.int32, (3, PAD, PIX), 0)
    column = lax.broadcasted_iota(jnp.int32, (3, PAD, PIX), 2)
    select = jnp.where(place - 9 + shift == column, 1.0, 0.0).astype(BF)
    select = select.reshape(3 * PAD, PIX)

    def widen(kind, row, scale):
        turned = dot_nt(select, raw[kind, row])
        if scale is not None:
            turned = turned * scale
        turned = turned.astype(BF)
        for offset in range(3):
            wide[offset, kind, row] = turned[offset * PAD : (offset + 1) * PAD]

    loads[0].wait()
    loads[1].wait()

    def widen_own(row, carry):
        widen(0, row + 2, None)
        widen(1, row + 2, None)
        return carry

    lax.fori_loop(0, ROWS, widen_own, 0)

    last = pl.ds(PIX, 16)
    early = pl.ds(0, 16)
    own = pl.ds(2, ROWS)
    side_copies = [
        send(4, wide.at[1, :, own, last], side.at[0, :, own], 0, 1),
        send(5, wide.at[1, :, own, early], side.at[1, :, own], 0, -1),
        send(6, wide.at[1, :, pl.ds(8, 2), last], side.at[0, :, pl.ds(0, 2)], 1, 1),
        send(7, wide.at[1, :, pl.ds(8, 2), early], side.at[1, :, pl.ds(0, 2)], 1, -1),
        send(8, wide.at[1, :, pl.ds(2, 2), last], side.at[0, :, pl.ds(10, 2)], -1, 1),
        send(9, wide.at[1, :, pl.ds(2, 2), early], side.at[1, :, pl.ds(10, 2)], -1, -1),
    ]

    above = jnp.where(s > 0, 1.0, 0.0).astype(F32)
    below = jnp.where(s < n_slab - 1, 1.0, 0.0).astype(F32)
    leftward = jnp.where(c > 0, 1.0, 0.0).astype(F32)
    rightward = jnp.where(c < n_chan - 1, 1.0, 0.0).astype(F32)

    for copy in row_copies:
        copy.wait()

    def widen_halo(kind, carry):
        for row in (0, 1):
            widen(kind, row, above)
        for row in (10, 11):
            widen(kind, row, below)
        return carry

    lax.fori_loop(0, 2, widen_halo, 0)

    for copy in side_copies:
        copy.wait()
    lane_row = lax.broadcasted_iota(jnp.int32, (16, C), 0)
    edge = (lane_row == 7) | (lane_row == 8)

    def patch(row, carry):
        inside = jnp.where(row < 2, above, jnp.where(row > 9, below, 1.0))
        for kind in range(2):
            low = side[0, kind, row].astype(F32) * (inside * leftward)
            high = side[1, kind, row].astype(F32) * (inside * rightward)
            tile = wide[1, kind, row, 0:16].astype(F32)
            wide[1, kind, row, 0:16] = jnp.where(lane_row < 8, low, tile).astype(BF)
            tile = wide[0, kind, row, 0:16].astype(F32)
            wide[0, kind, row, 0:16] = jnp.where(edge, pltpu.roll(low, 1, 0), tile).astype(BF)
            tile = wide[1, kind, row, PIX:PAD].astype(F32)
            wide[1, kind, row, PIX:PAD] = jnp.where(lane_row >= 8, high, tile).astype(BF)
            tile = wide[2, kind, row, PIX:PAD].astype(F32)
            wide[2, kind, row, PIX:PAD] = jnp.where(edge, pltpu.roll(high, 15, 0), tile).astype(BF)
        return carry

    lax.fori_loop(0, ROWS + 4, patch, 0)

    loads[2].wait()
    n1 = 5

    def layer_one(part, carry):
        base = part * n1
        center = jnp.zeros((n1 * PAD, C), F32)
        radius = jnp.zeros((n1 * PAD, C), F32)
        for a in range(3):
            for b in range(3):
                weight = first[a, b]
                mid_in = wide[b, 0, pl.ds(base + a, n1)].reshape(n1 * PAD, C)
                rad_in = wide[b, 1, pl.ds(base + a, n1)].reshape(n1 * PAD, C)
                center = center + dot_nt(mid_in, weight)
                radius = radius + dot_nt(rad_in, jnp.abs(weight))
        middle, spread = interval_relu(center + first_bias[...], radius)
        row_at = lax.broadcasted_iota(jnp.int32, (n1, PAD, C), 0) + base + (s * ROWS - 1)
        col_at = lax.broadcasted_iota(jnp.int32, (n1, PAD, C), 1) + (c * PIX - 8)
        inside = (
            (row_at >= 0)
            & (row_at < n_slab * ROWS)
            & (col_at >= 0)
            & (col_at < n_chan * PIX)
        )
        middle = jnp.where(inside, middle.reshape(n1, PAD, C), 0.0)
        spread = jnp.where(inside, spread.reshape(n1, PAD, C), 0.0)
        for b in range(3):
            layer[b, 0, pl.ds(base, n1)] = middle[:, 7 + b : 7 + b + PIX].astype(BF)
            layer[b, 1, pl.ds(base, n1)] = spread[:, 7 + b : 7 + b + PIX].astype(BF)
        return carry

    lax.fori_loop(0, 2, layer_one, 0)

    for load in loads[3:]:
        load.wait()

    def layer_two(read, count):
        center = jnp.zeros((count * PIX, C), F32)
        radius = jnp.zeros((count * PIX, C), F32)
        for a in range(3):
            for b in range(3):
                weight = second[a, b]
                center = center + dot_nt(read(b, 0, a), weight)
                radius = radius + dot_nt(read(b, 1, a), jnp.abs(weight))
        middle, spread = interval_relu(center + second_bias[...], radius)
        return middle.astype(BF), spread.astype(BF)

    def head(middle, spread, weight, bias):
        return dot_nt(middle, weight) + bias, dot_nt(spread, jnp.abs(weight))

    first_row = tile_row[0, 0]
    second_row = tile_row[0, 1]

    def read_tiles(b, kind, a):
        return jnp.concatenate(
            [layer[b, kind, first_row + a], layer[b, kind, second_row + a]], axis=0
        )

    middle_two, radius_two = layer_two(read_tiles, 2)
    pre_three = head(middle_two, radius_two, third[...], third_bias[...])
    slope_three, offset_three = relax_slopes(*pre_three)
    middle_three, radius_three = interval_relu(*pre_three)
    pre_four = head(
        middle_three.astype(BF), radius_three.astype(BF), fourth[...], fourth_bias[...]
    )
    slope_four, offset_four = relax_slopes(*pre_four)
    score = score_weight[...].astype(F32)
    coeff_four = (score * slope_four).astype(BF)
    carried = dot_nn(coeff_four, fourth[...])
    coeff_three = (carried * slope_three).astype(BF)
    reached = dot_nn(coeff_three, third[...])
    shared = (
        coeff_four.astype(F32) * fourth_bias[...]
        + coeff_three.astype(F32) * third_bias[...]
        + reached * middle_two.astype(F32)
    )
    reach = jnp.abs(reached) * radius_two.astype(F32)
    lower = (
        shared + jnp.minimum(score, 0.0) * offset_four + jnp.minimum(carried, 0.0) * offset_three
    ) - reach
    upper = (
        shared + jnp.maximum(score, 0.0) * offset_four + jnp.maximum(carried, 0.0) * offset_three
    ) + reach
    bias_score = score_bias[0, 0]

    def column_sum(value):
        halves = value[:, :PIX] + value[:, PIX:]
        return jnp.sum(halves.T, axis=0, keepdims=True) + bias_score

    sub = lax.broadcasted_iota(jnp.int32, (8, PIX), 0)
    blob = jnp.zeros((8, PIX), F32)
    for tile in range(2):
        rows = slice(tile * PIX, (tile + 1) * PIX)
        blob = jnp.where(sub == 2 * tile, column_sum(lower[rows]), blob)
        blob = jnp.where(sub == 2 * tile + 1, column_sum(upper[rows]), blob)
        slot = jnp.where(tile < tile_count[0, 0], owner_slot[0, tile], -1)
        blob = jnp.where(sub == 4 + tile, slot.astype(F32), blob)
    gathered[c] = blob

    def chan_copy(step):
        return pltpu.make_async_remote_copy(
            src_ref=gathered.at[c],
            dst_ref=gathered.at[c],
            send_sem=chan_send.at[step - 1],
            recv_sem=chan_recv.at[step - 1],
            device_id=(s, chan_at(step)),
            device_id_type=MESH,
        )

    def chan_start(step, carry):
        chan_copy(step).start()
        return carry

    def chan_wait(step, carry):
        chan_copy(step).wait()
        return carry

    lax.fori_loop(1, n_chan, chan_start, 0)

    n2 = 4
    score_rows = jnp.broadcast_to(score_weight[...], (16, C)).astype(BF)

    def forward(part):
        def read(b, kind, a):
            return layer[b, kind, pl.ds(part * n2 + a, n2)].reshape(n2 * PIX, C)

        middle, spread = layer_two(read, n2)
        middle, spread = interval_relu(*head(middle, spread, third[...], third_bias[...]))
        middle, spread = interval_relu(
            *head(middle.astype(BF), spread.astype(BF), fourth[...], fourth_bias[...])
        )
        center = dot_nt(score_rows, middle.astype(BF)) + bias_score
        radius = dot_nt(jnp.abs(score_rows), spread.astype(BF))
        low = (center - radius)[:8]
        high = (center + radius)[:8]
        for row in range(n2):
            cols = slice(row * PIX, (row + 1) * PIX)
            ibp_out[0, pl.ds(part * n2 + row, 1)] = low[0:1, cols]
            ibp_out[1, pl.ds(part * n2 + row, 1)] = high[0:1, cols]

    forward(0)

    lax.fori_loop(1, n_chan, chan_wait, 0)
    keeper = lax.broadcasted_iota(jnp.int32, (n_slab, PIX), 0).astype(F32) * 8.0

    def collect(peer, carry):
        low, high, slots = carry
        for tile in range(2):
            slot = gathered[peer, 4 + tile : 5 + tile]
            mine = (slot >= keeper) & (slot < keeper + 8.0)
            low = jnp.where(mine, gathered[peer, 2 * tile : 2 * tile + 1], low)
            high = jnp.where(mine, gathered[peer, 2 * tile + 1 : 2 * tile + 2], high)
            slots = jnp.where(mine, slot - keeper + 1.0, slots)
        return low, high, slots

    empty = jnp.zeros((n_slab, PIX), F32)
    low, high, slots = lax.fori_loop(0, n_chan, collect, (empty, empty, empty))
    message[:, 0, :] = low
    message[:, 1, :] = high
    message[:, 2, :] = slots
    arrived[s] = message[s]

    def slab_copy(step):
        return pltpu.make_async_remote_copy(
            src_ref=message.at[slab_at(step)],
            dst_ref=arrived.at[s],
            send_sem=slab_send.at[step - 1],
            recv_sem=slab_recv.at[step - 1],
            device_id=(slab_at(step), c),
            device_id_type=MESH,
        )

    def slab_start(step, carry):
        slab_copy(step).start()
        return carry

    def slab_wait(step, carry):
        slab_copy(step).wait()
        return carry

    lax.fori_loop(1, n_slab, slab_start, 0)

    forward(1)

    lax.fori_loop(1, n_slab, slab_wait, 0)
    wanted = lax.broadcasted_iota(jnp.int32, (8, PIX), 0).astype(F32) + 1.0

    def keep(peer, carry):
        low, high = carry
        mine = arrived[peer, 2:3] == wanted
        return (
            jnp.where(mine, arrived[peer, 0:1], low),
            jnp.where(mine, arrived[peer, 1:2], high),
        )

    empty = jnp.zeros((8, PIX), F32)
    low, high = lax.fori_loop(0, n_slab, keep, (empty, empty))
    refined_out[:, 0, :] = low
    refined_out[:, 1, :] = high


def solution(mesh):
    n_slab = mesh.shape["slab"]
    n_chan = mesh.shape["chan"]

    def body(
        image_center,
        image_radius,
        first_kernel,
        first_bias,
        second_kernel,
        second_bias,
        third_weight,
        third_bias,
        fourth_weight,
        fourth_bias,
        score_weight,
        score_bias,
        tile_count,
        tile_row,
        owner_slot,
    ):
        hbm = pl.BlockSpec(memory_space=pl.ANY)
        vmem = pl.BlockSpec(memory_space=pltpu.VMEM)
        smem = pl.BlockSpec(memory_space=pltpu.SMEM)
        dma = pltpu.SemaphoreType.DMA
        return pl.pallas_call(
            functools.partial(kernel, n_slab, n_chan),
            out_shape=(
                jax.ShapeDtypeStruct((2, ROWS, PIX), F32),
                jax.ShapeDtypeStruct((8, 2, PIX), F32),
            ),
            in_specs=[hbm] * 6 + [vmem] * 5 + [smem] * 4,
            out_specs=(vmem, vmem),
            scratch_shapes=[
                pltpu.VMEM((2, ROWS + 4, C, PIX), BF),
                pltpu.VMEM((3, 2, ROWS + 4, PAD, C), BF),
                pltpu.VMEM((2, 2, ROWS + 4, 16, C), BF),
                pltpu.VMEM((3, 2, ROWS + 2, PIX, C), BF),
                pltpu.VMEM((3, 3, C, C), BF),
                pltpu.VMEM((3, 3, C, C), BF),
                pltpu.VMEM((C, C), BF),
                pltpu.VMEM((C, C), BF),
                pltpu.VMEM((n_chan, 8, PIX), F32),
                pltpu.VMEM((n_slab, 3, PIX), F32),
                pltpu.VMEM((n_slab, 3, PIX), F32),
                dma((6,)),
                dma((10,)),
                dma((10,)),
                dma((n_chan - 1,)),
                dma((n_chan - 1,)),
                dma((n_slab - 1,)),
                dma((n_slab - 1,)),
            ],
            compiler_params=pltpu.CompilerParams(
                collective_id=0, has_side_effects=True, vmem_limit_bytes=56 * 1024 * 1024
            ),
        )(
            image_center,
            image_radius,
            first_kernel,
            second_kernel,
            third_weight,
            fourth_weight,
            first_bias[None, :],
            second_bias[None, :],
            third_bias[None, :],
            fourth_bias[None, :],
            score_weight[None, :],
            score_bias[None, :],
            tile_count,
            tile_row[0],
            owner_slot[0],
        )

    placed = (
        P("slab", None, "chan"),
        P("slab", None, "chan"),
        *(P(),) * 10,
        P("slab", "chan"),
        P("slab", "chan", None),
        P("slab", "chan", None),
    )
    return jax.shard_map(
        body,
        mesh=mesh,
        in_specs=placed,
        out_specs=(P(None, "slab", "chan"), P("slab", None, None)),
        check_vma=False,
    )
```

time: 157 us -> 53.1 us (0.34)
  the two profiles are of different devices: /device:TPU:32 before, /device:TPU:1 now
where the time goes in v1:
time: 53.1 us; the launch traced here: 52.8 us
  Pallas kernels  47 us (89%)
  local copies, waits for them, and re-layouts  3.81 us (7%)
  between operations  1.93 us (4%)
    pallas_call x1, Pallas kernels, body(): pl.pallas_call(functools.partial(kernel, n_slab, n_chan), out_shape=(jax....  47 us
    unnamed x2, local copies, waits for them, and re-layouts  2.59 us
    broadcast_in_dim x1, local copies, waits for them, and re-layouts, body(): score_weight[None, :]  1.22 us

profile of v1, /device:TPU:1, one launch (start us, length us, event | category | flops | bytes accessed | tf_op | source)
XLA Modules:
  0.0 52.8 jit_solution(16220260055731935956)
XLA Ops:
  1.9 1.2 %broadcast_in_dim.22.score_weight = bf16[1,256]{1,0:T(2,128)(2,1)} reshape(bf16[256]{0:T(256)(128)(2,1)} %param.25) | data formatting | bytes 1024 | tf_op jit(solution)/shard_map/broadcast_in_dim | solution.py:487
  3.1 47.0 %shard_map.158 = (f32[2,8,128]{2,1,0:T(8,128)}, f32[8,2,128]{2,1,0:T(2,128)}) custom-call(bf16[8,256,128]{2,1,0:T(8,128)(2,1)} %center_in.1, bf16[8,256,128]{2,1,0:T(8,128)(2,1)} %radius_in.1, bf16[3,3,256,256]{3,2,1,0:T(8,128)(2,1)} %first_in.1, bf16[3,3,256,256]{3,2,1,0:T(8,128)(2,1)} %second_in.1, bf16[256,256]{1,0:T(8,128)(2,1)} %third_in.1, ...), custom_call_target="tpu_custom_call" | custom-call | tf_op jit(solution)/shard_map/pallas_call | solution.py:445
  50.2 1.3 %copy.21 = f32[2,8,128]{2,1,0:T(8,128)} copy(f32[2,8,128]{2,1,0:T(8,128)} %get-tuple-element.4) | data formatting | bytes 16384
  51.5 1.3 %copy.22 = f32[8,2,128]{2,1,0:T(2,128)} copy(f32[8,2,128]{2,1,0:T(2,128)} %get-tuple-element.5) | data formatting | bytes 16384

commit v2 on v1

--- a/solution.py
+++ b/solution.py
@@ -56,10 +56,10 @@
     tile_count,
     tile_row,
     owner_slot,
-    ibp_out,
-    refined_out,
+    out,
     raw,
     wide,
+    edges,
     side,
     layer,
     first,
@@ -121,7 +121,6 @@
             )
     lax.fori_loop(1, n_chan, greet_chan, 0)
     lax.fori_loop(1, n_slab, greet_slab, 0)
-    pl.semaphore_wait(barrier, n_chan + n_slab + 2)
 
     def send(index, source, target, row_step, col_step):
         copy = pltpu.make_async_remote_copy(
@@ -135,11 +134,41 @@
         copy.start()
         return copy
 
+    slot = lax.broadcasted_iota(jnp.int32, (32, PIX), 0)
+    column = lax.broadcasted_iota(jnp.int32, (32, PIX), 1)
+    outer = jnp.where(column < 2, column, jnp.where(column >= PIX - 2, column + 18 - PIX, 99))
+
+    loads[0].wait()
+    loads[1].wait()
+
+    def pack(row, carry):
+        pick = jnp.where(outer + 2 * row == slot, 1.0, 0.0).astype(BF)
+        return tuple(
+            total + dot_nt(pick, raw[kind, row + 2]) for kind, total in enumerate(carry)
+        )
+
+    empty = jnp.zeros((32, C), F32)
+    packed = lax.fori_loop(0, ROWS, pack, (empty, empty))
+    for kind in range(2):
+        edges[0, kind] = packed[kind][:16].astype(BF)
+        edges[1, kind] = packed[kind][16:].astype(BF)
+
+    pl.semaphore_wait(barrier, n_chan + n_slab + 2)
     row_copies = [
         send(0, center_in.at[pl.ds(6, 2)], raw.at[0, pl.ds(0, 2)], 1, 0),
         send(1, center_in.at[pl.ds(0, 2)], raw.at[0, pl.ds(10, 2)], -1, 0),
         send(2, radius_in.at[pl.ds(6, 2)], raw.at[1, pl.ds(0, 2)], 1, 0),
         send(3, radius_in.at[pl.ds(0, 2)], raw.at[1, pl.ds(10, 2)], -1, 0),
+    ]
+    side_copies = [
+        send(4, edges.at[1], side.at[0, 1], 0, 1),
+        send(5, edges.at[0], side.at[1, 1], 0, -1),
+    ]
+    corner_copies = [
+        send(6, edges.at[1], side.at[0, 0], 1, 1),
+        send(7, edges.at[0], side.at[1, 0], 1, -1),
+        send(8, edges.at[1], side.at[0, 2], -1, 1),
+        send(9, edges.at[0], side.at[1, 2], -1, -1),
     ]
 
     place = lax.broadcasted_iota(jnp.int32, (3, PAD, PIX), 1)
@@ -156,34 +185,72 @@
         for offset in range(3):
             wide[offset, kind, row] = turned[offset * PAD : (offset + 1) * PAD]
 
-    loads[0].wait()
-    loads[1].wait()
-
     def widen_own(row, carry):
         widen(0, row + 2, None)
         widen(1, row + 2, None)
         return carry
 
     lax.fori_loop(0, ROWS, widen_own, 0)
-
-    last = pl.ds(PIX, 16)
-    early = pl.ds(0, 16)
-    own = pl.ds(2, ROWS)
-    side_copies = [
-        send(4, wide.at[1, :, own, last], side.at[0, :, own], 0, 1),
-        send(5, wide.at[1, :, own, early], side.at[1, :, own], 0, -1),
-        send(6, wide.at[1, :, pl.ds(8, 2), last], side.at[0, :, pl.ds(0, 2)], 1, 1),
-        send(7, wide.at[1, :, pl.ds(8, 2), early], side.at[1, :, pl.ds(0, 2)], 1, -1),
-        send(8, wide.at[1, :, pl.ds(2, 2), last], side.at[0, :, pl.ds(10, 2)], -1, 1),
-        send(9, wide.at[1, :, pl.ds(2, 2), early], side.at[1, :, pl.ds(10, 2)], -1, -1),
-    ]
 
     above = jnp.where(s > 0, 1.0, 0.0).astype(F32)
     below = jnp.where(s < n_slab - 1, 1.0, 0.0).astype(F32)
     leftward = jnp.where(c > 0, 1.0, 0.0).astype(F32)
     rightward = jnp.where(c < n_chan - 1, 1.0, 0.0).astype(F32)
 
-    for copy in row_copies:
+    line = lax.broadcasted_iota(jnp.int32, (16, C), 0)
+    both = (line == 7) | (line == 8)
+
+    def patch(row, group, line_at, scale):
+        turn = 24 - 2 * line_at
+        for kind in range(2):
+            low = side[0, group, kind].astype(F32) * (scale * leftward)
+            high = side[1, group, kind].astype(F32) * (scale * rightward)
+            for offset, cols, mask, source, step in (
+                (0, slice(0, 16), both, low, turn - 1),
+                (1, slice(0, 16), line == 7, low, turn - 2),
+                (1, slice(PIX, PAD), line == 8, high, turn),
+                (2, slice(PIX, PAD), both, high, turn - 1),
+            ):
+                moved = pltpu.roll(source, step % 16, 0)
+                tile = wide[offset, kind, row, cols].astype(F32)
+                wide[offset, kind, row, cols] = jnp.where(mask, moved, tile).astype(BF)
+
+    def patch_own(row, carry):
+        patch(row + 2, 1, row, 1.0)
+        return carry
+
+    def layer_one(read, count, row_of):
+        center = jnp.zeros((count * PAD, C), F32)
+        radius = jnp.zeros((count * PAD, C), F32)
+        for a in range(3):
+            for b in range(3):
+                weight = first[a, b]
+                center = center + dot_nt(read(b, 0, a).reshape(count * PAD, C), weight)
+                radius = radius + dot_nt(read(b, 1, a).reshape(count * PAD, C), jnp.abs(weight))
+        middle, spread = interval_relu(center + first_bias[...], radius)
+        row_at = row_of(lax.broadcasted_iota(jnp.int32, (count, PAD, C), 0)) + (s * ROWS - 1)
+        col_at = lax.broadcasted_iota(jnp.int32, (count, PAD, C), 1) + (c * PIX - 8)
+        inside = (
+            (row_at >= 0)
+            & (row_at < n_slab * ROWS)
+            & (col_at >= 0)
+            & (col_at < n_chan * PIX)
+        )
+        middle = jnp.where(inside, middle.reshape(count, PAD, C), 0.0)
+        spread = jnp.where(inside, spread.reshape(count, PAD, C), 0.0)
+        return middle, spread
+
+    for copy in side_copies:
+        copy.wait()
+    lax.fori_loop(0, ROWS, patch_own, 0)
+    loads[2].wait()
+
+    inner = layer_one(lambda b, kind, a: wide[b, kind, 2 + a : 8 + a], 6, lambda row: row + 2)
+    for kind in range(2):
+        for b in range(3):
+            layer[b, kind, 2:8] = inner[kind][:, 7 + b : 7 + b + PIX].astype(BF)
+
+    for copy in row_copies + corner_copies:
         copy.wait()
 
     def widen_halo(kind, carry):
@@ -195,59 +262,24 @@
 
     lax.fori_loop(0, 2, widen_halo, 0)
 
-    for copy in side_copies:
-        copy.wait()
-    lane_row = lax.broadcasted_iota(jnp.int32, (16, C), 0)
-    edge = (lane_row == 7) | (lane_row == 8)
-
-    def patch(row, carry):
-        inside = jnp.where(row < 2, above, jnp.where(row > 9, below, 1.0))
-        for kind in range(2):
-            low = side[0, kind, row].astype(F32) * (inside * leftward)
-            high = side[1, kind, row].astype(F32) * (inside * rightward)
-            tile = wide[1, kind, row, 0:16].astype(F32)
-            wide[1, kind, row, 0:16] = jnp.where(lane_row < 8, low, tile).astype(BF)
-            tile = wide[0, kind, row, 0:16].astype(F32)
-            wide[0, kind, row, 0:16] = jnp.where(edge, pltpu.roll(low, 1, 0), tile).astype(BF)
-            tile = wide[1, kind, row, PIX:PAD].astype(F32)
-            wide[1, kind, row, PIX:PAD] = jnp.where(lane_row >= 8, high, tile).astype(BF)
-            tile = wide[2, kind, row, PIX:PAD].astype(F32)
-            wide[2, kind, row, PIX:PAD] = jnp.where(edge, pltpu.roll(high, 15, 0), tile).astype(BF)
-        return carry
-
-    lax.fori_loop(0, ROWS + 4, patch, 0)
-
-    loads[2].wait()
-    n1 = 5
-
-    def layer_one(part, carry):
-        base = part * n1
-        center = jnp.zeros((n1 * PAD, C), F32)
-        radius = jnp.zeros((n1 * PAD, C), F32)
-        for a in range(3):
-            for b in range(3):
-                weight = first[a, b]
-                mid_in = wide[b, 0, pl.ds(base + a, n1)].reshape(n1 * PAD, C)
-                rad_in = wide[b, 1, pl.ds(base + a, n1)].reshape(n1 * PAD, C)
-                center = center + dot_nt(mid_in, weight)
-                radius = radius + dot_nt(rad_in, jnp.abs(weight))
-        middle, spread = interval_relu(center + first_bias[...], radius)
-        row_at = lax.broadcasted_iota(jnp.int32, (n1, PAD, C), 0) + base + (s * ROWS - 1)
-        col_at = lax.broadcasted_iota(jnp.int32, (n1, PAD, C), 1) + (c * PIX - 8)
-        inside = (
-            (row_at >= 0)
-            & (row_at < n_slab * ROWS)
-            & (col_at >= 0)
-            & (col_at < n_chan * PIX)
-        )
-        middle = jnp.where(inside, middle.reshape(n1, PAD, C), 0.0)
-        spread = jnp.where(inside, spread.reshape(n1, PAD, C), 0.0)
+    def patch_halo(row, carry):
+        patch(row, 0, row + 6, above)
+        patch(row + 10, 2, row, below)
+        return carry
+
+    lax.fori_loop(0, 2, patch_halo, 0)
+    outside = layer_one(
+        lambda b, kind, a: jnp.concatenate(
+            [wide[b, kind, a : a + 2], wide[b, kind, 8 + a : 10 + a]], axis=0
+        ),
+        4,
+        lambda row: jnp.where(row < 2, row, row + 6),
+    )
+    for kind in range(2):
         for b in range(3):
-            layer[b, 0, pl.ds(base, n1)] = middle[:, 7 + b : 7 + b + PIX].astype(BF)
-            layer[b, 1, pl.ds(base, n1)] = spread[:, 7 + b : 7 + b + PIX].astype(BF)
-        return carry
-
-    lax.fori_loop(0, 2, layer_one, 0)
+            rows = outside[kind][:, 7 + b : 7 + b + PIX].astype(BF)
+            layer[b, kind, 0:2] = rows[:2]
+            layer[b, kind, 8:10] = rows[2:]
 
     for load in loads[3:]:
         load.wait()
@@ -282,7 +314,7 @@
         middle_three.astype(BF), radius_three.astype(BF), fourth[...], fourth_bias[...]
     )
     slope_four, offset_four = relax_slopes(*pre_four)
-    score = score_weight[...].astype(F32)
+    score = score_weight[...].astype(F32).reshape(1, C)
     coeff_four = (score * slope_four).astype(BF)
     carried = dot_nn(coeff_four, fourth[...])
     coeff_three = (carried * slope_three).astype(BF)
@@ -335,29 +367,6 @@
 
     lax.fori_loop(1, n_chan, chan_start, 0)
 
-    n2 = 4
-    score_rows = jnp.broadcast_to(score_weight[...], (16, C)).astype(BF)
-
-    def forward(part):
-        def read(b, kind, a):
-            return layer[b, kind, pl.ds(part * n2 + a, n2)].reshape(n2 * PIX, C)
-
-        middle, spread = layer_two(read, n2)
-        middle, spread = interval_relu(*head(middle, spread, third[...], third_bias[...]))
-        middle, spread = interval_relu(
-            *head(middle.astype(BF), spread.astype(BF), fourth[...], fourth_bias[...])
-        )
-        center = dot_nt(score_rows, middle.astype(BF)) + bias_score
-        radius = dot_nt(jnp.abs(score_rows), spread.astype(BF))
-        low = (center - radius)[:8]
-        high = (center + radius)[:8]
-        for row in range(n2):
-            cols = slice(row * PIX, (row + 1) * PIX)
-            ibp_out[0, pl.ds(part * n2 + row, 1)] = low[0:1, cols]
-            ibp_out[1, pl.ds(part * n2 + row, 1)] = high[0:1, cols]
-
-    forward(0)
-
     lax.fori_loop(1, n_chan, chan_wait, 0)
     keeper = lax.broadcasted_iota(jnp.int32, (n_slab, PIX), 0).astype(F32) * 8.0
 
@@ -398,7 +407,29 @@
 
     lax.fori_loop(1, n_slab, slab_start, 0)
 
-    forward(1)
+    n2 = 4
+    score_rows = jnp.broadcast_to(score, (16, C)).astype(BF)
+
+    def forward(part, carry):
+        def read(b, kind, a):
+            return layer[b, kind, pl.ds(part * n2 + a, n2)].reshape(n2 * PIX, C)
+
+        middle, spread = layer_two(read, n2)
+        middle, spread = interval_relu(*head(middle, spread, third[...], third_bias[...]))
+        middle, spread = interval_relu(
+            *head(middle.astype(BF), spread.astype(BF), fourth[...], fourth_bias[...])
+        )
+        center = dot_nt(score_rows, middle.astype(BF)) + bias_score
+        radius = dot_nt(jnp.abs(score_rows), spread.astype(BF))
+        low = (center - radius)[:8]
+        high = (center + radius)[:8]
+        for row in range(n2):
+            cols = slice(row * PIX, (row + 1) * PIX)
+            out[pl.ds(part * n2 + row, 1)] = low[0:1, cols]
+            out[pl.ds(ROWS + part * n2 + row, 1)] = high[0:1, cols]
+        return carry
+
+    lax.fori_loop(0, 2, forward, 0)
 
     lax.fori_loop(1, n_slab, slab_wait, 0)
     wanted = lax.broadcasted_iota(jnp.int32, (8, PIX), 0).astype(F32) + 1.0
@@ -413,8 +444,15 @@
 
     empty = jnp.zeros((8, PIX), F32)
     low, high = lax.fori_loop(0, n_slab, keep, (empty, empty))
-    refined_out[:, 0, :] = low
-    refined_out[:, 1, :] = high
+    out[16:24] = low
+    out[24:32] = high
+
+
+def unpack(bounds, ibp_out, refined_out):
+    ibp_out[0] = bounds[0:8]
+    ibp_out[1] = bounds[8:16]
+    refined_out[:, 0, :] = bounds[16:24]
+    refined_out[:, 1, :] = bounds[24:32]
 
 
 def solution(mesh):
@@ -442,18 +480,16 @@
         vmem = pl.BlockSpec(memory_space=pltpu.VMEM)
         smem = pl.BlockSpec(memory_space=pltpu.SMEM)
         dma = pltpu.SemaphoreType.DMA
-        return pl.pallas_call(
+        bounds = pl.pallas_call(
             functools.partial(kernel, n_slab, n_chan),
-            out_shape=(
-                jax.ShapeDtypeStruct((2, ROWS, PIX), F32),
-                jax.ShapeDtypeStruct((8, 2, PIX), F32),
-            ),
+            out_shape=jax.ShapeDtypeStruct((32, PIX), F32),
             in_specs=[hbm] * 6 + [vmem] * 5 + [smem] * 4,
-            out_specs=(vmem, vmem),
+            out_specs=vmem,
             scratch_shapes=[
                 pltpu.VMEM((2, ROWS + 4, C, PIX), BF),
                 pltpu.VMEM((3, 2, ROWS + 4, PAD, C), BF),
-                pltpu.VMEM((2, 2, ROWS + 4, 16, C), BF),
+                pltpu.VMEM((2, 2, 16, C), BF),
+                pltpu.VMEM((2, 3, 2, 16, C), BF),
                 pltpu.VMEM((3, 2, ROWS + 2, PIX, C), BF),
                 pltpu.VMEM((3, 3, C, C), BF),
                 pltpu.VMEM((3, 3, C, C), BF),
@@ -484,12 +520,21 @@
             second_bias[None, :],
             third_bias[None, :],
             fourth_bias[None, :],
-            score_weight[None, :],
+            score_weight,
             score_bias[None, :],
             tile_count,
             tile_row[0],
             owner_slot[0],
         )
+        return pl.pallas_call(
+            unpack,
+            out_shape=(
+                jax.ShapeDtypeStruct((2, ROWS, PIX), F32),
+                jax.ShapeDtypeStruct((8, 2, PIX), F32),
+            ),
+            in_specs=[vmem],
+            out_specs=(vmem, vmem),
+        )(bounds)
 
     placed = (
         P("slab", None, "chan"),

time: 53.1 us -> 47.8 us (0.900)
  local copies, waits for them, and re-layouts: 3.81 us -> 0 us
  Pallas kernels: 47 us -> 45.6 us
    unnamed x2 -> x0, local copies, waits for them, and re-layouts: 2.59 us -> none
    pallas_call x1 -> x2, Pallas kernels: 47 us -> 45.6 us  [the longest x1 44.3 us: body(): pl.pallas_call(functools.partial(kernel, n_slab, n_chan), out_shape=jax.S...]
    broadcast_in_dim x1 -> x0, local copies, waits for them, and re-layouts: 1.22 us -> none  [body(): score_weight[None, :]]
where the time goes in v2:
time: 47.8 us; the launch traced here: 47.5 us
  Pallas kernels  45.6 us (95%)
  between operations  1.93 us (4%)
    pallas_call x1, Pallas kernels, body(): pl.pallas_call(functools.partial(kernel, n_slab, n_chan), out_shape=jax.S...  44.3 us
    pallas_call x1, Pallas kernels, body(): pl.pallas_call(unpack, out_shape=(jax.ShapeDtypeStruct((2, ROWS, PIX), F3...  1.33 us

profile of v2, /device:TPU:1, one launch (start us, length us, event | category | flops | bytes accessed | tf_op | source)
XLA Modules:
  0.0 47.5 jit_solution(12533067858841127438)
XLA Ops:
  1.9 44.3 %shard_map.158.bounds = f32[32,128]{1,0:T(8,128)} custom-call(bf16[8,256,128]{2,1,0:T(8,128)(2,1)} %center_in.1, bf16[8,256,128]{2,1,0:T(8,128)(2,1)} %radius_in.1, bf16[3,3,256,256]{3,2,1,0:T(8,128)(2,1)} %first_in.1, bf16[3,3,256,256]{3,2,1,0:T(8,128)(2,1)} %second_in.1, bf16[256,256]{1,0:T(8,128)(2,1)} %third_in.1, bf16[256,256]{1,0:T(8,128)(2,1)} %fourth_in.1, ...), custom_call_target="tpu_custom_call" | custom-call | tf_op jit(solution)/shard_map/pallas_call | solution.py:483
  46.2 1.3 %shard_map.159 = (f32[2,8,128]{2,1,0:T(8,128)}, f32[8,2,128]{2,1,0:T(2,128)}) custom-call(f32[32,128]{1,0:T(8,128)} %shard_map.158.bounds), custom_call_target="tpu_custom_call" | custom-call | tf_op jit(solution)/shard_map/pallas_call | solution.py:529

commit v3 on v2

--- a/solution.py
+++ b/solution.py
@@ -99,28 +99,21 @@
 
     barrier = pltpu.get_barrier_semaphore()
 
-    def greet_chan(step, carry):
+    def greet(row_step, col_step):
         pl.semaphore_signal(
-            barrier, inc=1, device_id=(s, chan_at(step)), device_id_type=MESH
-        )
-        return carry
-
-    def greet_slab(step, carry):
-        pl.semaphore_signal(
-            barrier, inc=1, device_id=(slab_at(step), c), device_id_type=MESH
-        )
-        return carry
+            barrier,
+            inc=1,
+            device_id=(slab_at(row_step), chan_at(col_step)),
+            device_id_type=MESH,
+        )
 
     for row_step in (-1, 1):
         for col_step in (-1, 1):
-            pl.semaphore_signal(
-                barrier,
-                inc=1,
-                device_id=(slab_at(row_step), chan_at(col_step)),
-                device_id_type=MESH,
-            )
-    lax.fori_loop(1, n_chan, greet_chan, 0)
-    lax.fori_loop(1, n_slab, greet_slab, 0)
+            greet(row_step, col_step)
+    for step in range(1, n_chan):
+        greet(0, step)
+    for step in range(1, n_slab):
+        greet(step, 0)
 
     def send(index, source, target, row_step, col_step):
         copy = pltpu.make_async_remote_copy(
@@ -357,17 +350,9 @@
             device_id_type=MESH,
         )
 
-    def chan_start(step, carry):
+    for step in range(1, n_chan):
         chan_copy(step).start()
-        return carry
-
-    def chan_wait(step, carry):
-        chan_copy(step).wait()
-        return carry
-
-    lax.fori_loop(1, n_chan, chan_start, 0)
-
-    lax.fori_loop(1, n_chan, chan_wait, 0)
+
     keeper = lax.broadcasted_iota(jnp.int32, (n_slab, PIX), 0).astype(F32) * 8.0
 
     def collect(peer, carry):
@@ -380,32 +365,43 @@
             slots = jnp.where(mine, slot - keeper + 1.0, slots)
         return low, high, slots
 
+    def collect_from(step, carry):
+        chan_copy(step).wait_recv()
+        return collect(chan_at(n_chan - step), carry)
+
     empty = jnp.zeros((n_slab, PIX), F32)
-    low, high, slots = lax.fori_loop(0, n_chan, collect, (empty, empty, empty))
+    found = collect(c, (empty, empty, empty))
+    low, high, slots = lax.fori_loop(1, n_chan, collect_from, found)
     message[:, 0, :] = low
     message[:, 1, :] = high
     message[:, 2, :] = slots
     arrived[s] = message[s]
 
-    def slab_copy(step):
+    def other(index):
+        return index + lax.div(index - s + n_slab, n_slab)
+
+    def slab_copy(index):
         return pltpu.make_async_remote_copy(
-            src_ref=message.at[slab_at(step)],
+            src_ref=message.at[other(index)],
             dst_ref=arrived.at[s],
-            send_sem=slab_send.at[step - 1],
-            recv_sem=slab_recv.at[step - 1],
-            device_id=(slab_at(step), c),
+            send_sem=slab_send.at[index],
+            recv_sem=slab_recv.at[s],
+            device_id=(other(index), c),
             device_id_type=MESH,
         )
 
-    def slab_start(step, carry):
-        slab_copy(step).start()
-        return carry
-
-    def slab_wait(step, carry):
-        slab_copy(step).wait()
-        return carry
-
-    lax.fori_loop(1, n_slab, slab_start, 0)
+    def slab_arrival(index):
+        return pltpu.make_async_remote_copy(
+            src_ref=message.at[other(index)],
+            dst_ref=arrived.at[other(index)],
+            send_sem=slab_send.at[index],
+            recv_sem=slab_recv.at[other(index)],
+            device_id=(other(index), c),
+            device_id_type=MESH,
+        )
+
+    for index in range(n_slab - 1):
+        slab_copy(index).start()
 
     n2 = 4
     score_rows = jnp.broadcast_to(score, (16, C)).astype(BF)
@@ -431,7 +427,6 @@
 
     lax.fori_loop(0, 2, forward, 0)
 
-    lax.fori_loop(1, n_slab, slab_wait, 0)
     wanted = lax.broadcasted_iota(jnp.int32, (8, PIX), 0).astype(F32) + 1.0
 
     def keep(peer, carry):
@@ -443,9 +438,25 @@
         )
 
     empty = jnp.zeros((8, PIX), F32)
-    low, high = lax.fori_loop(0, n_slab, keep, (empty, empty))
+
+    def keep_from(index, carry):
+        slab_arrival(index).wait_recv()
+        return keep(other(index), carry)
+
+    low, high = lax.fori_loop(0, n_slab - 1, keep_from, keep(s, (empty, empty)))
     out[16:24] = low
     out[24:32] = high
+
+    def chan_sent(step, carry):
+        chan_copy(step).wait_send()
+        return carry
+
+    def slab_sent(index, carry):
+        slab_copy(index).wait_send()
+        return carry
+
+    lax.fori_loop(1, n_chan, chan_sent, 0)
+    lax.fori_loop(0, n_slab - 1, slab_sent, 0)
 
 
 def unpack(bounds, ibp_out, refined_out):
@@ -504,7 +515,7 @@
                 dma((n_chan - 1,)),
                 dma((n_chan - 1,)),
                 dma((n_slab - 1,)),
-                dma((n_slab - 1,)),
+                dma((n_slab,)),
             ],
             compiler_params=pltpu.CompilerParams(
                 collective_id=0, has_side_effects=True, vmem_limit_bytes=56 * 1024 * 1024

time: 47.8 us -> 47.6 us (level)
  no operation moved by 1% of the time
where the time goes in v3:
time: 47.6 us; the launch traced here: 47.3 us
  Pallas kernels  45.4 us (95%)
  between operations  1.93 us (4%)
    pallas_call x1, Pallas kernels, body(): pl.pallas_call(functools.partial(kernel, n_slab, n_chan), out_shape=jax.S...  44.1 us
    pallas_call x1, Pallas kernels, body(): pl.pallas_call(unpack, out_shape=(jax.ShapeDtypeStruct((2, ROWS, PIX), F3...  1.33 us

profile of v3, /device:TPU:1, one launch (start us, length us, event | category | flops | bytes accessed | tf_op | source)
XLA Modules:
  0.0 47.3 jit_solution(17072929014712252094)
XLA Ops:
  1.9 44.1 %shard_map.158.bounds = f32[32,128]{1,0:T(8,128)} custom-call(bf16[8,256,128]{2,1,0:T(8,128)(2,1)} %center_in.1, bf16[8,256,128]{2,1,0:T(8,128)(2,1)} %radius_in.1, bf16[3,3,256,256]{3,2,1,0:T(8,128)(2,1)} %first_in.1, bf16[3,3,256,256]{3,2,1,0:T(8,128)(2,1)} %second_in.1, bf16[256,256]{1,0:T(8,128)(2,1)} %third_in.1, bf16[256,256]{1,0:T(8,128)(2,1)} %fourth_in.1, ...), custom_call_target="tpu_custom_call" | custom-call | tf_op jit(solution)/shard_map/pallas_call | solution.py:494
  46.0 1.3 %shard_map.159 = (f32[2,8,128]{2,1,0:T(8,128)}, f32[8,2,128]{2,1,0:T(2,128)}) custom-call(f32[32,128]{1,0:T(8,128)} %shard_map.158.bounds), custom_call_target="tpu_custom_call" | custom-call | tf_op jit(solution)/shard_map/pallas_call | solution.py:540

commit v4 on v3

--- a/solution.py
+++ b/solution.py
@@ -69,6 +69,7 @@
     gathered,
     message,
     arrived,
+    known,
     local_sem,
     halo_send,
     halo_recv,
@@ -107,13 +108,30 @@
             device_id_type=MESH,
         )
 
-    for row_step in (-1, 1):
-        for col_step in (-1, 1):
-            greet(row_step, col_step)
-    for step in range(1, n_chan):
-        greet(0, step)
-    for step in range(1, n_slab):
-        greet(step, 0)
+    for row_step in (-1, 0, 1):
+        for col_step in (-1, 0, 1):
+            if row_step or col_step:
+                greet(row_step, col_step)
+
+    rounds = []
+    distance = 1
+    while 2 * distance < max(n_slab, n_chan):
+        along = [(distance, 0), (-distance, 0)] if 2 * distance < n_slab else []
+        across = [(0, distance), (0, -distance)] if 2 * distance < n_chan else []
+        rounds.append(along + across)
+        distance *= 2
+
+    def tell(index):
+        for row_step, col_step in rounds[index]:
+            pl.semaphore_signal(
+                known.at[index],
+                inc=1,
+                device_id=(slab_at(row_step), chan_at(col_step)),
+                device_id_type=MESH,
+            )
+
+    def hear(index):
+        pl.semaphore_wait(known.at[index], len(rounds[index]))
 
     def send(index, source, target, row_step, col_step):
         copy = pltpu.make_async_remote_copy(
@@ -146,7 +164,7 @@
         edges[0, kind] = packed[kind][:16].astype(BF)
         edges[1, kind] = packed[kind][16:].astype(BF)
 
-    pl.semaphore_wait(barrier, n_chan + n_slab + 2)
+    pl.semaphore_wait(barrier, 8)
     row_copies = [
         send(0, center_in.at[pl.ds(6, 2)], raw.at[0, pl.ds(0, 2)], 1, 0),
         send(1, center_in.at[pl.ds(0, 2)], raw.at[0, pl.ds(10, 2)], -1, 0),
@@ -164,6 +182,8 @@
         send(9, edges.at[0], side.at[1, 2], -1, -1),
     ]
 
+    tell(0)
+
     place = lax.broadcasted_iota(jnp.int32, (3, PAD, PIX), 1)
     shift = lax.broadcasted_iota(jnp.int32, (3, PAD, PIX), 0)
     column = lax.broadcasted_iota(jnp.int32, (3, PAD, PIX), 2)
@@ -233,16 +253,22 @@
         spread = jnp.where(inside, spread.reshape(count, PAD, C), 0.0)
         return middle, spread
 
+    hear(0)
+    tell(1)
     for copy in side_copies:
         copy.wait()
     lax.fori_loop(0, ROWS, patch_own, 0)
     loads[2].wait()
+    hear(1)
+    tell(2)
 
     inner = layer_one(lambda b, kind, a: wide[b, kind, 2 + a : 8 + a], 6, lambda row: row + 2)
     for kind in range(2):
         for b in range(3):
             layer[b, kind, 2:8] = inner[kind][:, 7 + b : 7 + b + PIX].astype(BF)
 
+    hear(2)
+    tell(3)
     for copy in row_copies + corner_copies:
         copy.wait()
 
@@ -274,6 +300,7 @@
             layer[b, kind, 0:2] = rows[:2]
             layer[b, kind, 8:10] = rows[2:]
 
+    hear(3)
     for load in loads[3:]:
         load.wait()
 
@@ -509,6 +536,7 @@
                 pltpu.VMEM((n_chan, 8, PIX), F32),
                 pltpu.VMEM((n_slab, 3, PIX), F32),
                 pltpu.VMEM((n_slab, 3, PIX), F32),
+                pltpu.SemaphoreType.REGULAR((4,)),
                 dma((6,)),
                 dma((10,)),
                 dma((10,)),

time: 47.6 us -> 47.1 us (0.989)
  Pallas kernels: 45.4 us -> 44.9 us
    pallas_call x1, Pallas kernels: 44.1 us -> 43.5 us  [body(): pl.pallas_call(functools.partial(kernel, n_slab, n_chan), out_shape=jax.S...]
where the time goes in v4:
time: 47.1 us; the launch traced here: 46.8 us
  Pallas kernels  44.9 us (95%)
  between operations  1.93 us (4%)
    pallas_call x1, Pallas kernels, body(): pl.pallas_call(functools.partial(kernel, n_slab, n_chan), out_shape=jax.S...  43.5 us
    pallas_call x1, Pallas kernels, body(): pl.pallas_call(unpack, out_shape=(jax.ShapeDtypeStruct((2, ROWS, PIX), F3...  1.33 us

profile of v4, /device:TPU:1, one launch (start us, length us, event | category | flops | bytes accessed | tf_op | source)
XLA Modules:
  0.0 46.8 jit_solution(11745235332322185871)
XLA Ops:
  1.9 43.5 %shard_map.158.bounds = f32[32,128]{1,0:T(8,128)} custom-call(bf16[8,256,128]{2,1,0:T(8,128)(2,1)} %center_in.1, bf16[8,256,128]{2,1,0:T(8,128)(2,1)} %radius_in.1, bf16[3,3,256,256]{3,2,1,0:T(8,128)(2,1)} %first_in.1, bf16[3,3,256,256]{3,2,1,0:T(8,128)(2,1)} %second_in.1, bf16[256,256]{1,0:T(8,128)(2,1)} %third_in.1, bf16[256,256]{1,0:T(8,128)(2,1)} %fourth_in.1, ...), custom_call_target="tpu_custom_call" | custom-call | tf_op jit(solution)/shard_map/pallas_call | solution.py:521
  45.5 1.3 %shard_map.159 = (f32[2,8,128]{2,1,0:T(8,128)}, f32[8,2,128]{2,1,0:T(2,128)}) custom-call(f32[32,128]{1,0:T(8,128)} %shard_map.158.bounds), custom_call_target="tpu_custom_call" | custom-call | tf_op jit(solution)/shard_map/pallas_call | solution.py:568

commit v5 on v4

--- a/solution.py
+++ b/solution.py
@@ -454,6 +454,17 @@
 
     lax.fori_loop(0, 2, forward, 0)
 
+    def chan_sent(step, carry):
+        chan_copy(step).wait_send()
+        return carry
+
+    def slab_sent(index, carry):
+        slab_copy(index).wait_send()
+        return carry
+
+    lax.fori_loop(1, n_chan, chan_sent, 0)
+    lax.fori_loop(0, n_slab - 1, slab_sent, 0)
+
     wanted = lax.broadcasted_iota(jnp.int32, (8, PIX), 0).astype(F32) + 1.0
 
     def keep(peer, carry):
@@ -473,17 +484,6 @@
     low, high = lax.fori_loop(0, n_slab - 1, keep_from, keep(s, (empty, empty)))
     out[16:24] = low
     out[24:32] = high
-
-    def chan_sent(step, carry):
-        chan_copy(step).wait_send()
-        return carry
-
-    def slab_sent(index, carry):
-        slab_copy(index).wait_send()
-        return carry
-
-    lax.fori_loop(1, n_chan, chan_sent, 0)
-    lax.fori_loop(0, n_slab - 1, slab_sent, 0)
 
 
 def unpack(bounds, ibp_out, refined_out):

time: 47.1 us -> 46.7 us (level)
  no operation moved by 1% of the time
where the time goes in v5:
time: 46.7 us; the launch traced here: 46.5 us
  Pallas kernels  44.6 us (96%)
  between operations  1.93 us (4%)
    pallas_call x1, Pallas kernels, body(): pl.pallas_call(functools.partial(kernel, n_slab, n_chan), out_shape=jax.S...  43.2 us
    pallas_call x1, Pallas kernels, body(): pl.pallas_call(unpack, out_shape=(jax.ShapeDtypeStruct((2, ROWS, PIX), F3...  1.33 us

profile of v5, /device:TPU:1, one launch (start us, length us, event | category | flops | bytes accessed | tf_op | source)
XLA Modules:
  0.0 46.5 jit_solution(18370522651425355223)
XLA Ops:
  1.9 43.2 %shard_map.158.bounds = f32[32,128]{1,0:T(8,128)} custom-call(bf16[8,256,128]{2,1,0:T(8,128)(2,1)} %center_in.1, bf16[8,256,128]{2,1,0:T(8,128)(2,1)} %radius_in.1, bf16[3,3,256,256]{3,2,1,0:T(8,128)(2,1)} %first_in.1, bf16[3,3,256,256]{3,2,1,0:T(8,128)(2,1)} %second_in.1, bf16[256,256]{1,0:T(8,128)(2,1)} %third_in.1, bf16[256,256]{1,0:T(8,128)(2,1)} %fourth_in.1, ...), custom_call_target="tpu_custom_call" | custom-call | tf_op jit(solution)/shard_map/pallas_call | solution.py:521
  45.2 1.3 %shard_map.159 = (f32[2,8,128]{2,1,0:T(8,128)}, f32[8,2,128]{2,1,0:T(2,128)}) custom-call(f32[32,128]{1,0:T(8,128)} %shard_map.158.bounds), custom_call_target="tpu_custom_call" | custom-call | tf_op jit(solution)/shard_map/pallas_call | solution.py:568
